TPU v7x, 256 devices: a whole 4x4x8 slice. The times are simulated.
256 devices in a mesh: grp: 8 (over x, y_hi), mem: 32 (over y_lo, z, core).
Axes of the slice: x: 4, y: 4 (y_hi: 2, y_lo: 2; y = y_hi * 2 + y_lo), z: 8, core: 2. Of those that a mesh axis runs over, the one named last changes fastest.
Arguments:
- grad_tiles: bfloat16 [8, 16384, 1024], P(None, 'mem', 'grp'), may hold values from -0.59765625 to 0.59765625
- g_basis: bfloat16 [8, 16384, 1024], P(None, 'mem', 'grp'), may hold values from -0.1875 to 0.1875
- a_basis: bfloat16 [8, 1024, 1024], P(None, 'mem', 'grp'), may hold values from -0.1875 to 0.1875
- g_values: float32 [8, 16384], replicated, may hold values from 0.05 to 4
- a_values: float32 [8, 1024], replicated, may hold values from 0.05 to 4
- layer_group: int32 [8], replicated, may hold values from 0 to 7, as said below
- block_counts: int32 [8], replicated, may hold values from 1 to 16, as said below
Outputs:
- updates: bfloat16 [8, 3, 16384, 1024], P('grp', None, 'mem')
Inputs may be any that keep to these rules, and one draw needn't show every extreme that they name: `layer_group`: exactly one group receives 3 layers; every other group receives at most one. `block_counts`: some layer has all 16 blocks live.
All inputs are finite; a program needn't handle non-finite values.
Results may differ from a plain program's by a relative error of at most 0.006.
Values may be sent and summed in bfloat16 or wider, within the bound.
A program may use at most 64 MiB of HBM per device.

v0:
```python
import jax
import jax.numpy as jnp
from jax import lax
from jax.sharding import PartitionSpec as P

CAP = 3


DAMPING = 0.05


def from_partner(value, axis, stride):
    mask = 2**stride
    pairs = [(source, source ^ mask) for source in range(lax.axis_size(axis))]
    return lax.ppermute(value, axis, pairs)


def precondition(grad_rows, g_piece, a_piece, values_g, values_a, live_counts, side_bit, row_block):
    num_slots = grad_rows.shape[0]
    a_full = lax.all_gather(a_piece, "mem", axis=1, tiled=True)
    partner_g = from_partner(g_piece, "mem", 0)
    upper_part = jnp.where(side_bit == 0, g_piece, partner_g)
    lower_part = jnp.where(side_bit == 0, partner_g, g_piece)
    g_full = jnp.concatenate([upper_part, lower_part], axis=1)
    order = a_full.shape[1]
    half_width = order // 2
    block_values = lax.dynamic_slice_in_dim(values_g, row_block * order, order, 1)
    half_values = lax.dynamic_slice_in_dim(values_a, side_bit * half_width, half_width, 1)
    results = []
    for slot_index in range(num_slots):
        right_turned = jnp.dot(
            grad_rows[slot_index], a_full[slot_index], preferred_element_type=jnp.float32
        ).astype(jnp.bfloat16)
        own_cols = lax.dynamic_slice_in_dim(right_turned, side_bit * half_width, half_width, 1)
        outgoing = lax.dynamic_slice_in_dim(
            right_turned, (1 - side_bit) * half_width, half_width, 1
        )
        received = from_partner(outgoing, "mem", 0)
        turned_cols = jnp.where(
            side_bit == 0,
            jnp.concatenate([own_cols, received], axis=0),
            jnp.concatenate([received, own_cols], axis=0),
        )
        rotated = lax.dot_general(
            g_full[slot_index],
            turned_cols,
            (((0,), (0,)), ((), ())),
            preferred_element_type=jnp.float32,
        )
        denom = block_values[slot_index][:, None] * half_values[slot_index][None, :] + DAMPING
        scaled = (rotated / denom).astype(jnp.bfloat16)
        back_left = jnp.dot(g_full[slot_index], scaled, preferred_element_type=jnp.float32).astype(
            jnp.bfloat16
        )
        own_rows = lax.dynamic_slice_in_dim(back_left, side_bit * half_width, half_width, 0)
        outgoing_rows = lax.dynamic_slice_in_dim(
            back_left, (1 - side_bit) * half_width, half_width, 0
        )
        received_rows = from_partner(outgoing_rows, "mem", 0)
        turned_rows = jnp.where(
            side_bit == 0,
            jnp.concatenate([own_rows, received_rows], axis=1),
            jnp.concatenate([received_rows, own_rows], axis=1),
        )
        update = lax.dot_general(
            turned_rows,
            a_full[slot_index],
            (((1,), (1,)), ((), ())),
            preferred_element_type=jnp.float32,
        )
        update = jnp.where(row_block < live_counts[slot_index], update, jnp.float32(0.0)).astype(
            jnp.bfloat16
        )
        results.append(update)
    return jnp.stack(results, axis=0)


def local(grad_tiles, g_basis, a_basis, g_values, a_values, layer_group, block_counts):
    group_count = lax.axis_size("grp")
    group_index = lax.axis_index("grp")
    member = lax.axis_index("mem")
    side_bit = member % 2
    row_block = member // 2
    layer_total = layer_group.shape[0]
    positions = jnp.arange(layer_total)
    earlier = positions[None, :] < positions[:, None]
    same_group = layer_group[None, :] == layer_group[:, None]
    slot_rank = jnp.sum(jnp.logical_and(earlier, same_group), axis=1)
    group_match = layer_group[None, None, :] == jnp.arange(group_count)[:, None, None]
    rank_match = slot_rank[None, None, :] == jnp.arange(CAP)[None, :, None]
    slot_table = jnp.logical_and(group_match, rank_match)
    table_bf = slot_table.astype(jnp.bfloat16)

    def by_slots(source):
        picked = jnp.einsum(
            "dsl,lrc->dsrc", table_bf, source, preferred_element_type=jnp.float32
        ).astype(jnp.bfloat16)
        return picked.reshape(group_count * CAP, source.shape[1], source.shape[2])

    got_grad, got_g, got_a = (
        lax.all_to_all(by_slots(grad_tiles), "grp", split_axis=0, concat_axis=2, tiled=True),
        lax.all_to_all(by_slots(g_basis), "grp", split_axis=0, concat_axis=2, tiled=True),
        lax.all_to_all(by_slots(a_basis), "grp", split_axis=0, concat_axis=2, tiled=True),
    )
    own_table = lax.dynamic_index_in_dim(slot_table, group_index, 0, keepdims=False)
    own_weights = own_table.astype(jnp.float32)
    values_g = jnp.dot(own_weights, g_values, precision=lax.Precision.HIGHEST)
    values_a = jnp.dot(own_weights, a_values, precision=lax.Precision.HIGHEST)
    live_counts = jnp.sum(jnp.where(own_table, block_counts[None, :], 0), axis=1)
    result = precondition(
        got_grad, got_g, got_a, values_g, values_a, live_counts, side_bit, row_block
    )
    return result[None]


def solution(mesh):
    in_specs = (
        P(None, "mem", "grp"),
        P(None, "mem", "grp"),
        P(None, "mem", "grp"),
        P(),
        P(),
        P(),
        P(),
    )
    out_specs = P("grp", None, "mem", None)
    return jax.shard_map(local, mesh=mesh, in_specs=in_specs, out_specs=out_specs, check_vma=False)
```

profile of v0, /device:TPU:8, one launch (start us, length us, event | category | flops | bytes accessed | tf_op | source)
XLA Modules:
  0.0 189.6 jit_solution(1777032676931284645)
XLA Ops:
  6.5 1.0 convert_reduce_fusion
  7.5 0.7 iota_compare_fusion.1
  8.2 1.0 convolution_convert_fusion.5
  9.3 14.0 %all_to_all.51 = bf16[24,32,128]{2,1,0:T(8,128)(2,1)S(1)} all-to-all(bf16[24,32,128]{2,1,0:T(8,128)(2,1)S(1)} %bitcast.116), channel_id=1, replica_groups=mesh['grp'=8,'mem'=32] {'grp'}, dimensions={0} | all-to-all | bytes 393216 | tf_op jit(solution)/shard_map/all_to_all | solution.py:103
  23.3 0.8 all_to_all.47
  24.1 1.0 convolution_convert_fusion.1
  25.1 0.7 copy.47
  25.8 47.3 %all_to_all.52 = bf16[24,512,128]{2,1,0:T(8,128)(2,1)} all-to-all(bf16[24,512,128]{2,1,0:T(8,128)(2,1)S(1)} %bitcast.110), channel_id=1, replica_groups=mesh['grp'=8,'mem'=32] {'grp'}, dimensions={0} | all-to-all | bytes 6291456 | tf_op jit(solution)/shard_map/all_to_all | solution.py:102
  73.1 4.7 %copy.48 = bf16[3,512,8,128]{1,3,2,0:T(8,128)(2,1)} copy(bf16[3,512,8,128]{3,1,0,2:T(8,128)(2,1)} %bitcast.111) | data formatting | bytes 6291456 | tf_op jit(solution)/shard_map/all_to_all | solution.py:102
  77.8 1.0 convolution_convert_fusion
  78.8 2.4 %copy.50 = bf16[8,3,512,128]{3,2,1,0:T(8,128)(2,1)} copy(bf16[8,3,512,128]{3,0,2,1:T(8,128)(2,1)S(1)} %convolution_convert_fusion) | data formatting | bytes 6291456 | tf_op jit(solution)/shard_map/convert_element_type | solution.py:97
  81.2 4.6 %all-to-all-start.1 = ((bf16[24,512,128]{2,1,0:T(8,128)(2,1)}), bf16[24,512,128]{2,1,0:T(8,128)(2,1)}, u32[]{:S(2)}, u32[]{:S(2)}) async-start(bf16[24,512,128]{2,1,0:T(8,128)(2,1)} %bitcast.108), calls=%async_computation.1 | async-start | bytes 6291456 | tf_op jit(solution)/shard_map/all_to_all | solution.py:101
  89.1 43.2 %all-to-all-done.1 = bf16[24,512,128]{2,1,0:T(8,128)(2,1)} async-done(((bf16[24,512,128]{2,1,0:T(8,128)(2,1)}), bf16[24,512,128]{2,1,0:T(8,128)(2,1)}, u32[]{:S(2)}, u32[]{:S(2)}) %all-to-all-start.1) | async-done | bytes 3145760 | tf_op jit(solution)/shard_map/all_to_all | solution.py:101
  132.3 4.7 %copy.51 = bf16[8,3,512,128]{2,3,0,1:T(8,128)(2,1)} copy(bf16[8,3,512,128]{3,2,1,0:T(8,128)(2,1)} %bitcast.12) | data formatting | bytes 6291456 | tf_op jit(solution)/shard_map/all_to_all | solution.py:101
  137.0 3.3 %fusion.121 = (bf16[1,512,8,128]{1,3,2,0:T(8,128)(2,1)S(1)}, bf16[1,512,8,128]{1,3,2,0:T(8,128)(2,1)}, bf16[1,512,8,128]{1,3,2,0:T(8,128)(2,1)S(1)}) fusion(bf16[3,512,8,128]{1,3,2,0:T(8,128)(2,1)} %bitcast.109), kind=kLoop, calls=%fused_computation.145 | loop fusion | bytes 6291456 | tf_op jit(solution)/shard_map/slice | solution.py:32
  140.3 5.0 %broadcast_select_fusion.1 = (bf16[3,512,1024]{1,2,0:T(8,128)(2,1)}, bf16[3,512,1024]{1,2,0:T(8,128)(2,1)}) fusion(bf16[3,512,1024]{1,2,0:T(8,128)(2,1)} %collective-permute-done, pred[]{:T(512)S(6)} %eq.67, bf16[3,512,8,128]{1,3,2,0:T(8,128)(2,1)S(1)} %copy-done.2), kind=kLoop, calls=%fused_computation.6 | loop fusion | flops 3145728 | bytes 12582913 | tf_op jit(solution)/shard_map/jit(_where)/select_n | solution.py:22
  145.3 3.3 %fusion.11 = bf16[512,1024]{1,0:T(8,128)(2,1)S(1)} fusion(bf16[512,1024]{0,1:T(8,128)(2,1)} %bitcast.115, bf16[3,1024,1024]{2,1,0:T(8,128)(2,1)} %all-gather.2.cloned.1.call-done), kind=kOutput, calls=%fused_computation.30 | convolution fusion | flops 1074266112 | bytes 4194304 | tf_op jit(solution)/shard_map/dot_general | solution.py:31
  148.6 0.9 constant_dynamic-slice_fusion.5
  149.6 1.3 fusion.12
  150.9 0.9 constant_dynamic-slice_fusion.9
  152.3 1.3 fusion.13
  153.6 0.9 constant_dynamic-slice_fusion.13
  154.5 0.8 copy-done.9
  155.4 5.1 %convolution_convert_fusion.2 = bf16[1024,512]{0,1:T(8,128)(2,1)S(1)} fusion(bf16[3,512,1024]{1,2,0:T(8,128)(2,1)} %get-tuple-element.8, bf16[3,512,1024]{1,2,0:T(8,128)(2,1)} %get-tuple-element.7, bf16[512,512]{1,0:T(8,128)(2,1)} %copy-done.9, bf16[512,512]{1,0:T(8,128)(2,1)S(1)} %copy-done.5, f32[512]{0:T(512)S(1)} %bitcast.124, f32[1024]{0:T(1024)S(1)} %bitcast.121, ...), kind=kOutput, calls=%fused_computation.33 | convolution fusion | flops 2163212288 | bytes 8394753 | tf_op jit(solution)/shard_map/dot_general | solution.py:52
  161.2 5.2 %convolution_convert_fusion.3 = bf16[1024,512]{0,1:T(8,128)(2,1)S(1)} fusion(bf16[3,512,1024]{1,2,0:T(8,128)(2,1)} %get-tuple-element.7, bf16[3,512,1024]{1,2,0:T(8,128)(2,1)} %get-tuple-element.8, bf16[512,512]{1,0:T(8,128)(2,1)} %collective-permute-done.3, bf16[512,512]{1,0:T(8,128)(2,1)S(1)} %get-tuple-element.18, f32[512]{0:T(512)S(1)} %bitcast.123, ...), kind=kOutput, calls=%fused_computation.34 | convolution fusion | flops 2163212288 | bytes 14686209 | tf_op jit(solution)/shard_map/dot_general | solution.py:52
  166.4 0.9 constant_dynamic-slice_fusion.7
  167.4 5.0 %convolution_convert_fusion.4 = bf16[1024,512]{0,1:T(8,128)(2,1)S(1)} fusion(bf16[3,512,1024]{1,2,0:T(8,128)(2,1)} %get-tuple-element.7, bf16[3,512,1024]{1,2,0:T(8,128)(2,1)} %get-tuple-element.8, bf16[512,512]{1,0:T(8,128)(2,1)} %collective-permute-done.1, bf16[512,512]{1,0:T(8,128)(2,1)S(1)} %get-tuple-element.14, f32[512]{0:T(512)S(1)} %bitcast.122, ...), kind=kOutput, calls=%fused_computation.35 | convolution fusion | flops 2163212288 | bytes 14686209 | tf_op jit(solution)/shard_map/dot_general | solution.py:52
  172.5 0.8 collective-permute-start.2
  173.3 3.6 %fusion.16 = bf16[1,512,1024]{2,1,0:T(8,128)(2,1)S(1)} fusion(bf16[3,1024,1024]{2,1,0:T(8,128)(2,1)} %all-gather.2.cloned.1.call-done, bf16[512,512]{0,1:T(8,128)(2,1)} %collective-permute-done.6, bf16[512,512]{0,1:T(8,128)(2,1)S(1)} %get-tuple-element.20, pred[]{:T(512)S(6)} %lt.62, pred[]{:T(512)S(6)} %eq.67), kind=kOutput, calls=%fused_computation.38 | convolution fusion | flops 1079508992 | bytes 4194306 | tf_op jit(solution)/shard_map/dot_general | solution.py:65
  176.9 2.5 %fusion.15 = bf16[1,512,1024]{2,1,0:T(8,128)(2,1)S(1)} fusion(bf16[3,1024,1024]{2,1,0:T(8,128)(2,1)S(1)} %bitcast.126, bf16[512,512]{0,1:T(8,128)(2,1)} %collective-permute-done.4, bf16[512,512]{0,1:T(8,128)(2,1)S(1)} %get-tuple-element.16, pred[]{:T(512)S(6)} %lt.61, pred[]{:T(512)S(6)} %eq.67), kind=kOutput, calls=%fused_computation.37 | convolution fusion | flops 1079508992 | bytes 4194306 | tf_op jit(solution)/shard_map/dot_general | solution.py:65
  179.4 1.3 fusion.14
  180.8 2.0 %maximum_bitcast_fusion = bf16[1,3,512,1024]{3,2,1,0:T(8,128)(2,1)} fusion(bf16[1,512,1024]{2,1,0:T(8,128)(2,1)S(1)} %fusion.16, bf16[1,512,1024]{2,1,0:T(8,128)(2,1)S(1)} %fusion.15, bf16[1,512,1024]{2,1,0:T(8,128)(2,1)S(1)} %fusion.14), kind=kLoop, calls=%fused_computation.4 | loop fusion | flops 3145728 | bytes 6291456 | tf_op jit(solution)/shard_map/broadcast_in_dim | solution.py:113
  (53 shorter events, 3.0 us)
Async XLA Ops:
  6.5 82.1 %copy-start = (f32[8,16384]{1,0:T(8,128)S(1)}, f32[8,16384]{1,0:T(8,128)}, u32[]{:S(2)}) copy-start(f32[8,16384]{1,0:T(8,128)} %param.10) | copy-start | bytes 1572868
  6.5 17.6 %copy-start.3 = (bf16[8,512,128]{2,1,0:T(8,128)(2,1)S(1)}, bf16[8,512,128]{2,1,0:T(8,128)(2,1)}, u32[]{:S(2)}) copy-start(bf16[8,512,128]{2,1,0:T(8,128)(2,1)} %param.8) | copy-start | bytes 3145732
  6.5 138.8 %all-gather.2.cloned.1.call-start = ((), (), s32[]{:S(2)}) async-start(), calls=%async_computation.3 | async-start | bytes 6488064 | tf_op jit(solution)/shard_map/all_gather | solution.py:20
  73.1 4.7 %copy-start.4 = (bf16[8,512,128]{2,1,0:T(8,128)(2,1)S(1)}, bf16[8,512,128]{2,1,0:T(8,128)(2,1)}, u32[]{:S(2)}) copy-start(bf16[8,512,128]{2,1,0:T(8,128)(2,1)} %param.7) | copy-start | bytes 3145732
  77.8 62.4 %collective-permute-start = (bf16[3,512,1024]{1,2,0:T(8,128)(2,1)}, bf16[3,512,1024]{1,2,0:T(8,128)(2,1)}, u32[]{:S(2)}, u32[]{:S(2)}) collective-permute-start(bf16[3,512,1024]{1,2,0:T(8,128)(2,1)} %bitcast.112), channel_id=1, source_target_pairs={{0,1},{1,0},{2,3},{3,2},{4,5},{5,4},{6,7},{7,6},{8,9},{9,8},{10,11... | collective-permute-start | bytes 9437192 | tf_op jit(solution)/shard_map/ppermute | solution.py:15
  81.2 4.7 %copy-start.7 = (s32[8]{0:T(128)S(1)}, s32[8]{0:T(128)}, u32[]{:S(2)}) copy-start(s32[8]{0:T(128)} %param.13) | copy-start | bytes 100
  81.2 7.2 %copy-start.6 = (f32[8,1024]{1,0:T(8,128)S(1)}, f32[8,1024]{1,0:T(8,128)}, u32[]{:S(2)}) copy-start(f32[8,1024]{1,0:T(8,128)} %param.11) | copy-start | bytes 98308
  81.2 51.1 %all-to-all-start.1 = ((bf16[24,512,128]{2,1,0:T(8,128)(2,1)}), bf16[24,512,128]{2,1,0:T(8,128)(2,1)}, u32[]{:S(2)}, u32[]{:S(2)}) async-start(bf16[24,512,128]{2,1,0:T(8,128)(2,1)} %bitcast.108), calls=%async_computation.1 | async-start | bytes 6291456 | tf_op jit(solution)/shard_map/all_to_all | solution.py:101
  137.0 3.3 %copy-start.2 = (bf16[3,512,8,128]{1,3,2,0:T(8,128)(2,1)S(1)}, bf16[3,512,8,128]{1,3,2,0:T(8,128)(2,1)}, u32[]{:S(2)}) copy-start(bf16[3,512,8,128]{1,3,2,0:T(8,128)(2,1)} %copy.48) | copy-start | bytes 9437188
  145.3 4.3 %copy-start.8 = (bf16[3,1024,1024]{2,1,0:T(8,128)(2,1)S(1)}, bf16[3,1024,1024]{2,1,0:T(8,128)(2,1)}, u32[]{:S(2)}) copy-start(bf16[3,1024,1024]{2,1,0:T(8,128)(2,1)} %all-gather.2.cloned.1.call-done) | copy-start | bytes 18874372
  149.6 5.0 %collective-permute-start.5 = (bf16[512,512]{1,0:T(8,128)(2,1)S(1)}, bf16[512,512]{1,0:T(8,128)(2,1)S(1)}, u32[]{:S(2)}, u32[]{:S(2)}) collective-permute-start(bf16[512,512]{1,0:T(8,128)(2,1)S(1)} %get-tuple-element.23), channel_id=1, source_target_pairs={{0,1},{1,0},{2,3},{3,2},{4,5},{5,4},{6,7},{7,6},{8,9},{9,8},{10,11... | collective-permute-start | bytes 1572872 | tf_op jit(solution)/shard_map/ppermute | solution.py:15
  151.8 9.4 %collective-permute-start.3 = (bf16[512,512]{1,0:T(8,128)(2,1)}, bf16[512,512]{1,0:T(8,128)(2,1)}, u32[]{:S(2)}, u32[]{:S(2)}) collective-permute-start(bf16[512,512]{1,0:T(8,128)(2,1)} %get-tuple-element.19), channel_id=1, source_target_pairs={{0,1},{1,0},{2,3},{3,2},{4,5},{5,4},{6,7},{7,6},{8,9},{9,8},{10,11... | collective-permute-start | bytes 1572872 | tf_op jit(solution)/shard_map/ppermute | solution.py:15
  153.6 1.8 copy-start.5
  154.5 12.8 %collective-permute-start.1 = (bf16[512,512]{1,0:T(8,128)(2,1)}, bf16[512,512]{1,0:T(8,128)(2,1)}, u32[]{:S(2)}, u32[]{:S(2)}) collective-permute-start(bf16[512,512]{1,0:T(8,128)(2,1)} %get-tuple-element.15), channel_id=1, source_target_pairs={{0,1},{1,0},{2,3},{3,2},{4,5},{5,4},{6,7},{7,6},{8,9},{9,8},{10,11... | collective-permute-start | bytes 1572872 | tf_op jit(solution)/shard_map/ppermute | solution.py:15
  154.5 0.8 copy-start.9
  160.6 12.7 %collective-permute-start.6 = (bf16[512,512]{0,1:T(8,128)(2,1)S(1)}, bf16[512,512]{0,1:T(8,128)(2,1)}, u32[]{:S(2)}, u32[]{:S(2)}) collective-permute-start(bf16[512,512]{0,1:T(8,128)(2,1)S(1)} %get-tuple-element.21), channel_id=1, source_target_pairs={{0,1},{1,0},{2,3},{3,2},{4,5},{5,4},{6,7},{7,6},{8,9},{9,8},{10,11... | collective-permute-start | bytes 1572872 | tf_op jit(solution)/shard_map/ppermute | solution.py:15
  167.3 9.5 %collective-permute-start.4 = (bf16[512,512]{0,1:T(8,128)(2,1)}, bf16[512,512]{0,1:T(8,128)(2,1)}, u32[]{:S(2)}, u32[]{:S(2)}) collective-permute-start(bf16[512,512]{0,1:T(8,128)(2,1)} %get-tuple-element.17), channel_id=1, source_target_pairs={{0,1},{1,0},{2,3},{3,2},{4,5},{5,4},{6,7},{7,6},{8,9},{9,8},{10,11... | collective-permute-start | bytes 1572872 | tf_op jit(solution)/shard_map/ppermute | solution.py:15
  172.4 4.5 %slice-start = ((s8[6291456]{0:T(1024)(128)(4,1)}), s8[4194304]{0:T(1024)(128)(4,1)S(1)}, s32[]{:S(2)}) async-start(s8[6291456]{0:T(1024)(128)(4,1)} %bitcast.125), calls=%async_computation.4 | async-start | bytes 8388608
  172.5 6.9 %collective-permute-start.2 = (bf16[512,512]{0,1:T(8,128)(2,1)S(1)}, bf16[512,512]{0,1:T(8,128)(2,1)S(1)}, u32[]{:S(2)}, u32[]{:S(2)}) collective-permute-start(bf16[512,512]{0,1:T(8,128)(2,1)S(1)} %get-tuple-element.13), channel_id=1, source_target_pairs={{0,1},{1,0},{2,3},{3,2},{4,5},{5,4},{6,7},{7,6},{8,9},{9,8},{10,11... | collective-permute-start | bytes 1572872 | tf_op jit(solution)/shard_map/ppermute | solution.py:15
  173.3 3.6 %slice-start.1 = ((s8[6291456]{0:T(1024)(128)(4,1)}), s8[2097152]{0:T(1024)(128)(4,1)S(1)}, s32[]{:S(2)}) async-start(s8[6291456]{0:T(1024)(128)(4,1)} %bitcast.125), calls=%async_computation.5 | async-start | bytes 4194304
  179.4 3.4 %copy-start.1 = (f32[8,16384]{1,0:T(8,128)S(1)}, f32[8,16384]{1,0:T(8,128)}, u32[]{:S(2)}) copy-start(f32[8,16384]{1,0:T(8,128)} %param.10) | copy-start | bytes 1572868
Sparse Core Ops, SparseCore 0:
  24.2 114.4 all-gather.1
where the time goes:
time: 192 us; the launch traced here: 190 us
  blocking collectives  61.3 us (32%)
  waiting for transfers between devices  43.2 us (22%)
  matrix products  32 us (17%)
  local copies, waits for them, and re-layouts  22.2 us (12%)
  between operations  15.5 us (8%)
  other arithmetic  8.81 us (5%)
  starting transfers between devices  6.52 us (3%)
    all_to_all x1, blocking collectives, local(): lax.all_to_all(by_slots(g_basis), 'grp', split_axis=0, concat_axis=2, til...  47.3 us
    all_to_all x1, waiting for transfers between devices, local(): lax.all_to_all(by_slots(grad_tiles), 'grp', split_axis=0, concat_axis=2,...  43.2 us
    dot_general x3, matrix products, precondition(): jnp.dot(g_full[slot_index], scaled, preferred_element_type=jnp.float32)  15.3 us
    all_to_all x1, blocking collectives, local(): lax.all_to_all(by_slots(a_basis), 'grp', split_axis=0, concat_axis=2, til...  14 us
    dot_general x3, matrix products, precondition(): lax.dot_general(turned_rows, a_full[slot_index], (((1,), (1,)), ((), ()))...  7.38 us
    dot_general x3, matrix products, precondition(): jnp.dot(grad_rows[slot_index], a_full[slot_index], preferred_element_type...  5.91 us
    select_n x1, other arithmetic, precondition(): upper_part = jnp.where(side_bit == 0, g_piece, partner_g)  5.04 us
    all_to_all x1, local copies, waits for them, and re-layouts, local(): lax.all_to_all(by_slots(g_basis), 'grp', split_axis=0, concat_axis=2, til...  4.73 us
  transfers between devices with their start and end apart: 9, of which 1 were waited for; matrix products, arithmetic and copies ran while one was open for 27% of the time, Pallas kernels for 0%

commit v1 on v0

v1 whole, which is shorter than its diff:
```python
import functools

import jax
import jax.numpy as jnp
import numpy as np
from jax import lax
from jax.experimental import pallas as pl
from jax.experimental.pallas import tpu as pltpu
from jax.sharding import PartitionSpec as P

CAP = 3
DAMPING = 0.05
MESH = pl.DeviceIdType.MESH
F32, BF16 = jnp.float32, jnp.bfloat16

NX, NY, NYL, NZ = 4, 2, 2, 8
PEERS = [(2, 0), (2, 1), (1, 0), (3, 0), (0, 1), (1, 1), (3, 1)]
CHUNK = 128
STEPS = 13
PIECE = 16


def return_tables():
    moves = {0: (1, 0), 1: (-1, 0), 2: (0, 1)}
    routes = {
        (1, 0): [(1,), (0, 0, 0), (2, 1, 2)],
        (2, 0): [(1, 1), (0, 0), (2, 1, 1, 2)],
        (0, 1): [(2,), (0, 2, 1), (1, 2, 0)],
        (1, 1): [(1, 2), (2, 1), (0, 0, 2, 0)],
        (2, 1): [(1, 1, 2), (2, 1, 1), (0, 2, 0)],
    }
    flip = {0: 1, 1: 0, 2: 2}
    for y in (0, 1):
        routes[(3, y)] = [tuple(flip[h] for h in r) for r in routes[(1, y)]]
    relay = np.zeros((8, 8), np.int32)
    info = np.zeros((8, 8), np.int32)
    for (ex, ey), paths in routes.items():
        row = ex * 2 + ey
        hops = [0, 0, 0]
        leads = [0, 0, 0]
        for path in paths:
            x, y = ex, ey
            for n, hop in enumerate(path):
                if n:
                    relay[row, x * 2 + y] = path[n - 1]
                x, y = (x + moves[hop][0]) % NX, (y + moves[hop][1]) % NY
            assert (x, y) == (0, 0)
            hops[path[-1]] = len(path)
            leads[path[0]] = path[-1]
        info[row, 0:3] = hops
        info[row, 3:6] = leads
    return np.concatenate([relay, info], axis=1).reshape(-1)


def kernel(
    lg, bc, tab, g_in, q_in, a_in, gv, av, out,
    stage_g, stage_q, stage_a, got_g, got_q, a_full, q_full, r_full, inv, s_ref, b_full,
    x_own, ret_out, ret_in,
    x_ss, x_rs, a_ss, a_rs, yl_s, zs_s, zr_s, sib_ss, sib_rs, qr_ss, qr_rs, b_s, ret_ss, ret_rs,
):
    grp = lax.axis_index("grp")
    mem = lax.axis_index("mem")
    x, yh = grp // 2, grp % 2
    yl, z, core = mem // 16, (mem // 2) % 8, mem % 2
    half, blk = s_ref.shape[1], s_ref.shape[0]
    n_grp = NX * NY

    def peer(dx, dy):
        return {"grp": ((x + dx) % NX) * 2 + (yh + dy) % NY, "mem": mem}

    def mate(dyl, dz, dc):
        row = ((yl + dyl) % NYL) * 16 + ((z + dz) % NZ) * 2 + (core + dc) % 2
        return {"grp": grp, "mem": row}

    sib = mate(0, 0, 1)

    def send(src, dst, ss, rs, device):
        return pltpu.make_async_remote_copy(
            src_ref=src, dst_ref=dst, send_sem=ss, recv_sem=rs,
            device_id=device, device_id_type=MESH,
        )

    barrier = pltpu.get_barrier_semaphore()
    greet = [peer(dx, dy) for dx, dy in PEERS]
    greet += [sib, mate(1, 0, 0), mate(0, 1, 0), mate(0, -1, 0)]
    for device in greet:
        pl.semaphore_signal(barrier, inc=1, device_id=device, device_id_type=MESH)

    def pick(cond, value):
        return jnp.where(cond, jnp.int32(value) if isinstance(value, int) else value, jnp.int32(0))

    group = [lg[l] for l in range(n_grp)]
    rank = [
        functools.reduce(lambda s, k: s + pick(group[k] == group[l], 1), range(l), jnp.int32(0))
        for l in range(n_grp)
    ]
    second, third, top, tx, ty = [jnp.int32(0)] * 5
    for l in range(n_grp):
        second = second + pick(rank[l] == 1, l)
        third = third + pick(rank[l] == 2, l)
        top = top + pick(rank[l] == 2, group[l])
    for i in range(n_grp):
        tx = tx + pick(top == i, i // NY)
        ty = ty + pick(top == i, i % NY)
    layer, empties = [], jnp.int32(0)
    helper, helper_x, helper_y = ([jnp.int32(0)] * 2 for _ in range(3))
    my_layer, my_has, my_count = jnp.int32(0), jnp.int32(0), jnp.int32(0)
    for i in range(n_grp):
        count, first = jnp.int32(0), jnp.int32(0)
        for l in range(n_grp):
            here = group[l] == i
            count = count + pick(here, 1)
            first = first + pick(jnp.logical_and(here, rank[l] == 0), l)
        empty = count == 0
        layer.append(jnp.where(empty, jnp.where(empties == 0, second, third), first))
        for e in range(2):
            chosen = jnp.logical_and(empty, empties == e)
            helper[e] = helper[e] + pick(chosen, i)
            helper_x[e] = helper_x[e] + pick(chosen, i // NY)
            helper_y[e] = helper_y[e] + pick(chosen, i % NY)
        empties = empties + pick(empty, 1)
        my_layer = my_layer + pick(grp == i, layer[i])
        my_has = my_has + pick(grp == i, jnp.where(empty, jnp.int32(0), jnp.int32(1)))
    for l in range(n_grp):
        my_count = my_count + pick(my_layer == l, bc[l])
    live = my_count > mem // 2

    for i in range(n_grp):
        stage_a[i] = a_in[layer[i]]
    pl.semaphore_wait(barrier, len(greet))

    a_rows = a_in.shape[1]
    cols = g_in.shape[2]
    my_cols = pl.ds(pl.multiple_of(grp * cols, cols), cols)

    def piece(yl_, z_, core_):
        start = ((yl_ % NYL) * 16 + (z_ % NZ) * 2 + core_) * a_rows
        return pl.ds(pl.multiple_of(start, a_rows), a_rows)

    own_piece = piece(yl, z, core)
    a_copies = []
    for n, (dx, dy) in enumerate(PEERS):
        device = peer(dx, dy)
        a_copies.append(send(stage_a.at[device["grp"]], a_full.at[own_piece, my_cols],
                             a_ss.at[n], a_rs.at[n], device))
        a_copies[-1].start()
    a_full[own_piece, my_cols] = stage_a[grp]

    n_chunk = g_in.shape[1] // CHUNK
    x_copies = []
    for c in range(n_chunk):
        rows = pl.ds(c * CHUNK, CHUNK)
        for i in range(n_grp):
            stage_g[i, rows] = g_in[layer[i], rows]
            stage_q[i, rows] = q_in[layer[i], rows]
        for n, (dx, dy) in enumerate(PEERS):
            device = peer(dx, dy)
            for t, (src, dst) in enumerate(((stage_g, got_g), (stage_q, got_q))):
                copy = send(src.at[device["grp"], rows], dst.at[grp, rows],
                            x_ss.at[c, t, n], x_rs.at[c, t, n], device)
                copy.start()
                x_copies.append(copy)
        got_g[grp, rows] = stage_g[grp, rows]
        got_q[grp, rows] = stage_q[grp, rows]

    pending = []
    sib_copies = []

    def to_sib(rows):
        n = len(sib_copies)
        copy = send(a_full.at[rows], a_full.at[rows], sib_ss.at[n], sib_rs.at[n], sib)
        copy.start()
        sib_copies.append(copy)

    def along_z(way, step, j, rows):
        copy = send(a_full.at[rows], a_full.at[rows], zs_s.at[way, step, j], zr_s.at[way, step, j],
                    mate(0, 1 - 2 * way, 0))
        copy.start()
        pending.append(copy)
        return copy

    for copy in a_copies:
        copy.wait_recv()
    ring = {}
    over_y = send(a_full.at[own_piece], a_full.at[own_piece], yl_s.at[0], yl_s.at[1], mate(1, 0, 0))
    over_y.start()
    for way in range(2):
        ring[way, 0, 0] = along_z(way, 0, 0, own_piece)
    to_sib(own_piece)

    my_half = pl.ds(pl.multiple_of(core * half, half), half)
    block_row = pl.ds(pl.multiple_of((mem // 2) * blk, blk), blk)
    e_row, a_row = gv[0:1, block_row], av[0:1, my_half]
    for l in range(1, n_grp):
        e_row = jnp.where(my_layer == l, gv[l:l + 1, block_row], e_row)
        a_row = jnp.where(my_layer == l, av[l:l + 1, my_half], a_row)
    for t in range(blk // 128):
        tile = jnp.broadcast_to(e_row[:, t * 128:(t + 1) * 128], (128, 128)).T
        for u in range(half // 128):
            denom = tile * a_row[:, u * 128:(u + 1) * 128] + DAMPING
            inv[t * 128:(t + 1) * 128, u * 128:(u + 1) * 128] = 1.0 / denom

    over_y.wait_recv()
    other_piece = piece(yl + 1, z, core)
    for way in range(2):
        ring[way, 0, 1] = along_z(way, 0, 1, other_piece)
    to_sib(other_piece)
    for step in range(1, 5):
        for j in range(2):
            for way in range(2):
                if (way, step - 1, j) not in ring:
                    continue
                ring[way, step - 1, j].wait_recv()
                came = piece(yl + j, z - step * (1 - 2 * way), core)
                if step < 3 or (step == 3 and j == way):
                    ring[way, step, j] = along_z(way, step, j, came)
                to_sib(came)
    for copy in sib_copies:
        copy.wait_recv()

    qr_copies = []
    sib_half = pl.ds(pl.multiple_of((1 - core) * half, half), half)
    for c in range(n_chunk):
        rows = pl.ds(c * CHUNK, CHUNK)
        abs_rows = pl.ds(pl.multiple_of(core * half + c * CHUNK, CHUNK), CHUNK)
        for copy in x_copies[c * 14:(c + 1) * 14]:
            copy.wait_recv()
        q_full[abs_rows, :] = jnp.concatenate([got_q[i, rows] for i in range(n_grp)], axis=1)
        copy = send(q_full.at[abs_rows], q_full.at[abs_rows], qr_ss.at[0, c], qr_rs.at[0, c], sib)
        copy.start()
        qr_copies.append(copy)
        g_rows = jnp.concatenate([got_g[i, rows] for i in range(n_grp)], axis=1)
        for n in range(blk // 256):
            r_full[abs_rows, n * 256:(n + 1) * 256] = jnp.dot(
                g_rows, a_full[:, n * 256:(n + 1) * 256], preferred_element_type=F32
            ).astype(BF16)
        copy = send(r_full.at[abs_rows, sib_half], r_full.at[abs_rows, sib_half],
                    qr_ss.at[1, c], qr_rs.at[1, c], sib)
        copy.start()
        qr_copies.append(copy)
    for copy in qr_copies:
        copy.wait_recv()

    for t in range(blk // 256):
        rotated = lax.dot_general(q_full[:, t * 256:(t + 1) * 256], r_full[:, my_half],
                                  (((0,), (0,)), ((), ())), preferred_element_type=F32)
        s_ref[t * 256:(t + 1) * 256, :] = (rotated * inv[t * 256:(t + 1) * 256, :]).astype(BF16)

    b_copies = []
    for t in range(4):
        who = 1 - core if t < 2 else core
        rows = pl.ds(pl.multiple_of(who * half + (t % 2) * 256, 256), 256)
        b_full[rows, my_half] = jnp.dot(
            q_full[rows, :], s_ref[...], preferred_element_type=F32
        ).astype(BF16)
        if t < 2:
            copy = send(b_full.at[rows, my_half], b_full.at[rows, my_half], b_s.at[0, t],
                        b_s.at[1, t], sib)
            copy.start()
            b_copies.append(copy)
    for copy in b_copies:
        copy.wait_recv()

    for t in range(half // 128):
        rows = pl.ds(pl.multiple_of(core * half + t * 128, 128), 128)
        left = b_full[rows, :]
        for n in range(blk // 256):
            update = lax.dot_general(left, a_full[n * 256:(n + 1) * 256, :],
                                     (((1,), (1,)), ((), ())), preferred_element_type=F32)
            update = jnp.where(live, update, 0.0).astype(BF16)
            per = 128 // PIECE
            x_own[t * per:(t + 1) * per, :, n * 256:(n + 1) * 256] = update.reshape(per, PIECE, 256)

    def apart(a, b, n):
        return jnp.where(a < b, a - b + n, a - b)

    here = apart(x, tx, NX) * 2 + apart(yh, ty, NY)
    is_helper, relay, base, lead, hops = [], [], [], [], []
    for e in range(2):
        row = (apart(helper_x[e], tx, NX) * 2 + apart(helper_y[e], ty, NY)) * 16
        is_helper.append(grp == helper[e])
        relay.append(tab[row + here])
        hops.append([tab[row + 8 + i] for i in range(3)])
        lead.append([tab[row + 11 + i] for i in range(3)])
        n0 = STEPS + 1 - hops[e][0]
        base.append([jnp.int32(0), n0, n0 + STEPS + 1 - hops[e][1]])
    n_piece = half // PIECE
    ways = [peer(1, 0), peer(-1, 0), peer(0, 1)]

    def ret_copy(e, step, o):
        return send(ret_out.at[e, step, o], ret_in.at[e, step, o], ret_ss.at[e, step % 2, o],
                    ret_rs.at[e, step, o], ways[o])

    def ret_step(step, first):
        for e in range(2):
            if not first:
                for o in range(3):
                    ret_copy(e, step - 1, o).wait_recv()
                carried = jnp.where(relay[e] == 0, ret_in[e, step - 1, 0],
                                    jnp.where(relay[e] == 1, ret_in[e, step - 1, 1],
                                              ret_in[e, step - 1, 2]))
            for o in range(3):
                start = jnp.where(lead[e][o] == 0, base[e][0],
                                  jnp.where(lead[e][o] == 1, base[e][1], base[e][2]))
                mine = x_own[jnp.minimum(start + step, n_piece - 1)]
                if not first:
                    mine = jnp.where(is_helper[e], mine, carried)
                ret_out[e, step, o] = mine
                if not first:
                    @pl.when(step >= 2)
                    def _():
                        ret_copy(e, step - 2, o).wait_send()
                ret_copy(e, step, o).start()

    ret_step(0, True)

    @pl.loop(1, STEPS)
    def _(step):
        ret_step(step, False)

    keep = my_has > 0
    for j in range(n_piece):
        value = x_own[j]
        out[0, j * PIECE:(j + 1) * PIECE, :] = jnp.where(keep, value, jnp.zeros_like(value))
    for e in range(2):
        for o in range(3):
            ret_copy(e, STEPS - 1, o).wait_recv()
    mine = grp == top
    for e in range(2):
        for j in range(n_piece):
            o = jnp.where(base[e][1] > j, 0, jnp.where(base[e][2] > j, 1, 2))
            start = jnp.where(o == 0, base[e][0], jnp.where(o == 1, base[e][1], base[e][2]))
            hop = jnp.where(o == 0, hops[e][0], jnp.where(o == 1, hops[e][1], hops[e][2]))
            value = ret_in[e, jnp.clip(j - start + hop - 1, 0, STEPS - 1), o]
            out[1 + e, j * PIECE:(j + 1) * PIECE, :] = jnp.where(mine, value, jnp.zeros_like(value))

    for e in range(2):
        for step in (STEPS - 2, STEPS - 1):
            for o in range(3):
                ret_copy(e, step, o).wait_send()
    for copy in a_copies + x_copies + [over_y] + pending + sib_copies + qr_copies + b_copies:
        copy.wait_send()


def local(grad_tiles, g_basis, a_basis, g_values, a_values, layer_group, block_counts):
    layers, rows, cols = grad_tiles.shape
    blk = 2 * rows
    dma = pltpu.SemaphoreType.DMA
    vmem = pl.BlockSpec(memory_space=pltpu.VMEM)
    smem = pl.BlockSpec(memory_space=pltpu.SMEM)
    n_chunk = rows // CHUNK
    result = pl.pallas_call(
        kernel,
        name="precondition",
        out_shape=jax.ShapeDtypeStruct((CAP, rows, blk), BF16),
        in_specs=[smem] * 3 + [vmem] * 5,
        out_specs=vmem,
        scratch_shapes=[
            pltpu.VMEM((layers, rows, cols), BF16),
            pltpu.VMEM((layers, rows, cols), BF16),
            pltpu.VMEM(a_basis.shape, BF16),
            pltpu.VMEM((layers, rows, cols), BF16),
            pltpu.VMEM((layers, rows, cols), BF16),
            pltpu.VMEM((blk, blk), BF16),
            pltpu.VMEM((blk, blk), BF16),
            pltpu.VMEM((blk, blk), BF16),
            pltpu.VMEM((blk, rows), F32),
            pltpu.VMEM((blk, rows), BF16),
            pltpu.VMEM((blk, blk), BF16),
            pltpu.VMEM((rows // PIECE, PIECE, blk), BF16),
            pltpu.VMEM((2, STEPS, 3, PIECE, blk), BF16),
            pltpu.VMEM((2, STEPS, 3, PIECE, blk), BF16),
            dma((n_chunk, 2, 7)), dma((n_chunk, 2, 7)),
            dma((7,)), dma((7,)),
            dma((2,)),
            dma((2, 4, 2)), dma((2, 4, 2)),
            dma((16,)), dma((16,)),
            dma((2, n_chunk)), dma((2, n_chunk)),
            dma((2, 2)),
            dma((2, 2, 3)), dma((2, STEPS, 3)),
        ],
        compiler_params=pltpu.CompilerParams(
            collective_id=0, has_side_effects=True, vmem_limit_bytes=48 * 1024 * 1024
        ),
    )(layer_group, block_counts, jnp.asarray(return_tables()), grad_tiles, g_basis, a_basis,
      g_values, a_values)
    return result[None]


def solution(mesh):
    in_specs = (
        P(None, "mem", "grp"),
        P(None, "mem", "grp"),
        P(None, "mem", "grp"),
        P(),
        P(),
        P(),
        P(),
    )
    out_specs = P("grp", None, "mem", None)
    return jax.shard_map(local, mesh=mesh, in_specs=in_specs, out_specs=out_specs, check_vma=False)
```

time: 192 us -> 123 us (0.64)
  Pallas kernels: 0 us -> 113 us
  blocking collectives: 61.3 us -> 0 us
  waiting for transfers between devices: 43.2 us -> 0 us
  matrix products: 32 us -> 0 us
  between operations: 15.5 us -> 0.02 us
  local copies, waits for them, and re-layouts: 22.2 us -> 8.72 us
  other arithmetic: 8.81 us -> 0 us
  starting transfers between devices: 6.52 us -> 0 us
    pallas_call x0 -> x1, Pallas kernels: none -> 113 us  [local(): pl.pallas_call(kernel, name='precondition', out_shape=jax.ShapeDtypeStruc...]
    all_to_all x2 -> x0, blocking collectives: 61.3 us -> none  [the longest x1 47.3 us: local(): lax.all_to_all(by_slots(g_basis), 'grp', split_axis=0, concat_axis=2, til...]
    all_to_all x1 -> x0, waiting for transfers between devices: 43.2 us -> none  [local(): lax.all_to_all(by_slots(grad_tiles), 'grp', split_axis=0, concat_axis=2,...]
    dot_general x14 -> x0, matrix products: 32 us -> none  [the longest x3 15.3 us: precondition(): jnp.dot(g_full[slot_index], scaled, preferred_element_type=jnp.float32)]
    all_to_all x4 -> x0, local copies, waits for them, and re-layouts: 10.3 us -> none  [the longest x1 4.73 us: local(): lax.all_to_all(by_slots(g_basis), 'grp', split_axis=0, concat_axis=2, til...]
    unnamed x24 -> x17, local copies, waits for them, and re-layouts: 0.88 us -> 8.72 us
    select_n x1 -> x0, other arithmetic: 5.04 us -> none  [precondition(): upper_part = jnp.where(side_bit == 0, g_piece, partner_g)]
    all_to_all x1 -> x0, starting transfers between devices: 4.6 us -> none  [local(): lax.all_to_all(by_slots(grad_tiles), 'grp', split_axis=0, concat_axis=2,...]
  transfers between devices with their start and end apart: 9 -> 0, of which waited for: 1 -> 0; matrix products, arithmetic and copies ran while one was open for 27% -> 0% of each run, Pallas kernels for 0% -> 0%
where the time goes in v1:
time: 123 us; the launch traced here: 122 us
  Pallas kernels  113 us (92%)
  local copies, waits for them, and re-layouts  8.72 us (7%)
    pallas_call x1, Pallas kernels, local(): pl.pallas_call(kernel, name='precondition', out_shape=jax.ShapeDtypeStruc...  113 us
    unnamed x17, local copies, waits for them, and re-layouts  8.72 us

profile of v1, /device:TPU:8, one launch (start us, length us, event | category | flops | bytes accessed | tf_op | source)
XLA Modules:
  0.0 121.8 jit_solution(16734900814022560487)
XLA Ops:
  0.0 0.0 copy-start
  0.0 1.2 %copy-done = bf16[8,512,128]{2,1,0:T(8,128)(2,1)S(1)} copy-done((bf16[8,512,128]{2,1,0:T(8,128)(2,1)S(1)}, bf16[8,512,128]{2,1,0:T(8,128)(2,1)}, u32[]{:S(2)}) %copy-start) | copy-done | bytes 1048600
  1.2 0.0 copy-start.1
  1.2 1.2 %copy-done.1 = bf16[8,512,128]{2,1,0:T(8,128)(2,1)S(1)} copy-done((bf16[8,512,128]{2,1,0:T(8,128)(2,1)S(1)}, bf16[8,512,128]{2,1,0:T(8,128)(2,1)}, u32[]{:S(2)}) %copy-start.1) | copy-done | bytes 1048600
  2.5 0.0 copy-start.2
  2.5 1.0 copy-done.2
  3.5 0.0 copy-start.3
  3.5 0.8 copy-done.3
  4.3 0.0 copy-start.4
  4.3 0.8 copy-done.4
  5.1 0.0 copy-start.5
  5.1 0.7 copy-done.5
  5.7 0.0 copy-start.6
  5.7 0.7 copy-done.6
  6.4 0.0 copy-start.7
  6.4 0.7 copy-done.7
  7.1 113.1 %precondition.1 = bf16[3,512,1024]{2,1,0:T(8,128)(2,1)S(1)} custom-call(s32[8]{0:T(128)S(1)} %copy-done.5, s32[8]{0:T(128)S(1)} %copy-done.6, s32[128]{0:T(128)S(1)} %copy-done.7, bf16[8,512,128]{2,1,0:T(8,128)(2,1)S(1)} %copy-done, bf16[8,512,128]{2,1,0:T(8,128)(2,1)S(1)} %copy-done.1, bf16[8,32,128]{2,1,0:T(8,128)(2,1)S(1)} %copy-done.3, ...), custom_call_target="tpu_custom_call" | custom-call | tf_op jit(solution)/shard_map/precondition/pallas_call | solution.py:352
  120.2 1.7 %copy.10 = bf16[1,3,512,1024]{3,2,1,0:T(8,128)(2,1)} copy(bf16[1,3,512,1024]{3,2,1,0:T(8,128)(2,1)S(1)} %bitcast.1) | data formatting | bytes 6291456
Async XLA Ops:
  0.0 1.2 %copy-start = (bf16[8,512,128]{2,1,0:T(8,128)(2,1)S(1)}, bf16[8,512,128]{2,1,0:T(8,128)(2,1)}, u32[]{:S(2)}) copy-start(bf16[8,512,128]{2,1,0:T(8,128)(2,1)} %g_in.1) | copy-start | bytes 3145732
  1.2 1.2 %copy-start.1 = (bf16[8,512,128]{2,1,0:T(8,128)(2,1)S(1)}, bf16[8,512,128]{2,1,0:T(8,128)(2,1)}, u32[]{:S(2)}) copy-start(bf16[8,512,128]{2,1,0:T(8,128)(2,1)} %q_in.1) | copy-start | bytes 3145732
  2.5 1.0 copy-start.2
  3.5 0.8 copy-start.3
  4.3 0.8 copy-start.4
  5.1 0.7 copy-start.5
  5.7 0.7 copy-start.6
  6.4 0.7 copy-start.7

commit v2 on v1

--- a/solution.py
+++ b/solution.py
@@ -16,7 +16,9 @@
 NX, NY, NYL, NZ = 4, 2, 2, 8
 PEERS = [(2, 0), (2, 1), (1, 0), (3, 0), (0, 1), (1, 1), (3, 1)]
 CHUNK = 128
-STEPS = 13
+LAG = 3
+STEPS = 17
+WHEN = [1, 2, 3, 4, 5, 6, 7, 8, 8, 8, 8]
 PIECE = 16
 
 
@@ -53,7 +55,8 @@
 
 
 def kernel(
-    lg, bc, tab, g_in, q_in, a_in, gv, av, out,
+    lg_hbm, bc_hbm, tab_hbm, g_hbm, q_hbm, a_hbm, gv_hbm, av_hbm, out_hbm,
+    lg, bc, tab, g_in, q_in, a_in, gv, av, out, in_sem, out_sem,
     stage_g, stage_q, stage_a, got_g, got_q, a_full, q_full, r_full, inv, s_ref, b_full,
     x_own, ret_out, ret_in,
     x_ss, x_rs, a_ss, a_rs, yl_s, zs_s, zr_s, sib_ss, sib_rs, qr_ss, qr_rs, b_s, ret_ss, ret_rs,
@@ -85,6 +88,17 @@
     greet += [sib, mate(1, 0, 0), mate(0, 1, 0), mate(0, -1, 0)]
     for device in greet:
         pl.semaphore_signal(barrier, inc=1, device_id=device, device_id_type=MESH)
+
+    block_row = pl.ds(pl.multiple_of((mem // 2) * blk, blk), blk)
+    my_half = pl.ds(pl.multiple_of(core * half, half), half)
+    loads = []
+    for n, (src, dst) in enumerate((
+        (lg_hbm, lg), (a_hbm, a_in), (g_hbm, g_in), (q_hbm, q_in), (bc_hbm, bc), (tab_hbm, tab),
+        (gv_hbm.at[:, block_row], gv), (av_hbm.at[:, my_half], av),
+    )):
+        loads.append(pltpu.make_async_copy(src, dst, in_sem.at[n]))
+        loads[-1].start()
+    loads[0].wait()
 
     def pick(cond, value):
         return jnp.where(cond, jnp.int32(value) if isinstance(value, int) else value, jnp.int32(0))
@@ -104,7 +118,7 @@
         ty = ty + pick(top == i, i % NY)
     layer, empties = [], jnp.int32(0)
     helper, helper_x, helper_y = ([jnp.int32(0)] * 2 for _ in range(3))
-    my_layer, my_has, my_count = jnp.int32(0), jnp.int32(0), jnp.int32(0)
+    my_layer, my_has = jnp.int32(0), jnp.int32(0)
     for i in range(n_grp):
         count, first = jnp.int32(0), jnp.int32(0)
         for l in range(n_grp):
@@ -121,10 +135,7 @@
         empties = empties + pick(empty, 1)
         my_layer = my_layer + pick(grp == i, layer[i])
         my_has = my_has + pick(grp == i, jnp.where(empty, jnp.int32(0), jnp.int32(1)))
-    for l in range(n_grp):
-        my_count = my_count + pick(my_layer == l, bc[l])
-    live = my_count > mem // 2
-
+    loads[1].wait()
     for i in range(n_grp):
         stage_a[i] = a_in[layer[i]]
     pl.semaphore_wait(barrier, len(greet))
@@ -148,20 +159,26 @@
 
     n_chunk = g_in.shape[1] // CHUNK
     x_copies = []
-    for c in range(n_chunk):
-        rows = pl.ds(c * CHUNK, CHUNK)
-        for i in range(n_grp):
-            stage_g[i, rows] = g_in[layer[i], rows]
-            stage_q[i, rows] = q_in[layer[i], rows]
-        for n, (dx, dy) in enumerate(PEERS):
-            device = peer(dx, dy)
-            for t, (src, dst) in enumerate(((stage_g, got_g), (stage_q, got_q))):
-                copy = send(src.at[device["grp"], rows], dst.at[grp, rows],
+    moves = ((g_in, stage_g, got_g, loads[2]), (q_in, stage_q, got_q, loads[3]))
+
+    def exchange(upto):
+        while len(x_copies) < 7 * upto:
+            c, t = divmod(len(x_copies) // 7, 2)
+            whole, stage, got, load = moves[t]
+            if c == 0:
+                load.wait()
+            rows = pl.ds(c * CHUNK, CHUNK)
+            for i in range(n_grp):
+                stage[i, rows] = whole[layer[i], rows]
+            for n, (dx, dy) in enumerate(PEERS):
+                device = peer(dx, dy)
+                copy = send(stage.at[device["grp"], rows], got.at[grp, rows],
                             x_ss.at[c, t, n], x_rs.at[c, t, n], device)
                 copy.start()
                 x_copies.append(copy)
-        got_g[grp, rows] = stage_g[grp, rows]
-        got_q[grp, rows] = stage_q[grp, rows]
+            got[grp, rows] = stage[grp, rows]
+
+    exchange(WHEN[0])
 
     pending = []
     sib_copies = []
@@ -187,13 +204,18 @@
     for way in range(2):
         ring[way, 0, 0] = along_z(way, 0, 0, own_piece)
     to_sib(own_piece)
-
-    my_half = pl.ds(pl.multiple_of(core * half, half), half)
-    block_row = pl.ds(pl.multiple_of((mem // 2) * blk, blk), blk)
-    e_row, a_row = gv[0:1, block_row], av[0:1, my_half]
+    exchange(WHEN[1])
+    for load in loads[4:]:
+        load.wait()
+    my_count = jnp.int32(0)
+    for l in range(n_grp):
+        my_count = my_count + pick(my_layer == l, bc[l])
+    live = my_count > mem // 2
+
+    e_row, a_row = gv[0:1, :], av[0:1, :]
     for l in range(1, n_grp):
-        e_row = jnp.where(my_layer == l, gv[l:l + 1, block_row], e_row)
-        a_row = jnp.where(my_layer == l, av[l:l + 1, my_half], a_row)
+        e_row = jnp.where(my_layer == l, gv[l:l + 1, :], e_row)
+        a_row = jnp.where(my_layer == l, av[l:l + 1, :], a_row)
     for t in range(blk // 128):
         tile = jnp.broadcast_to(e_row[:, t * 128:(t + 1) * 128], (128, 128)).T
         for u in range(half // 128):
@@ -205,6 +227,7 @@
     for way in range(2):
         ring[way, 0, 1] = along_z(way, 0, 1, other_piece)
     to_sib(other_piece)
+    exchange(WHEN[2])
     for step in range(1, 5):
         for j in range(2):
             for way in range(2):
@@ -215,6 +238,7 @@
                 if step < 3 or (step == 3 and j == way):
                     ring[way, step, j] = along_z(way, step, j, came)
                 to_sib(came)
+            exchange(WHEN[1 + 2 * step + j])
     for copy in sib_copies:
         copy.wait_recv()
 
@@ -282,60 +306,67 @@
         relay.append(tab[row + here])
         hops.append([tab[row + 8 + i] for i in range(3)])
         lead.append([tab[row + 11 + i] for i in range(3)])
-        n0 = STEPS + 1 - hops[e][0]
-        base.append([jnp.int32(0), n0, n0 + STEPS + 1 - hops[e][1]])
+        n0 = STEPS - LAG * (hops[e][0] - 1)
+        base.append([jnp.int32(0), n0, n0 + STEPS - LAG * (hops[e][1] - 1)])
     n_piece = half // PIECE
     ways = [peer(1, 0), peer(-1, 0), peer(0, 1)]
 
     def ret_copy(e, step, o):
-        return send(ret_out.at[e, step, o], ret_in.at[e, step, o], ret_ss.at[e, step % 2, o],
+        return send(ret_out.at[e, step, o], ret_in.at[e, step, o], ret_ss.at[e, step % LAG, o],
                     ret_rs.at[e, step, o], ways[o])
 
     def ret_step(step, first):
         for e in range(2):
             if not first:
                 for o in range(3):
-                    ret_copy(e, step - 1, o).wait_recv()
-                carried = jnp.where(relay[e] == 0, ret_in[e, step - 1, 0],
-                                    jnp.where(relay[e] == 1, ret_in[e, step - 1, 1],
-                                              ret_in[e, step - 1, 2]))
+                    ret_copy(e, step - LAG, o).wait_recv()
+                carried = jnp.where(relay[e] == 0, ret_in[e, step - LAG, 0],
+                                    jnp.where(relay[e] == 1, ret_in[e, step - LAG, 1],
+                                              ret_in[e, step - LAG, 2]))
             for o in range(3):
                 start = jnp.where(lead[e][o] == 0, base[e][0],
                                   jnp.where(lead[e][o] == 1, base[e][1], base[e][2]))
                 mine = x_own[jnp.minimum(start + step, n_piece - 1)]
                 if not first:
                     mine = jnp.where(is_helper[e], mine, carried)
+                    ret_copy(e, step - LAG, o).wait_send()
                 ret_out[e, step, o] = mine
-                if not first:
-                    @pl.when(step >= 2)
-                    def _():
-                        ret_copy(e, step - 2, o).wait_send()
                 ret_copy(e, step, o).start()
 
-    ret_step(0, True)
-
-    @pl.loop(1, STEPS)
-    def _(step):
-        ret_step(step, False)
+    for step in range(LAG):
+        ret_step(step, True)
 
     keep = my_has > 0
     for j in range(n_piece):
         value = x_own[j]
         out[0, j * PIECE:(j + 1) * PIECE, :] = jnp.where(keep, value, jnp.zeros_like(value))
-    for e in range(2):
-        for o in range(3):
-            ret_copy(e, STEPS - 1, o).wait_recv()
+    stores = [pltpu.make_async_copy(out.at[0], out_hbm.at[0], out_sem.at[0])]
+    stores[0].start()
+
+    @pl.loop(LAG, STEPS)
+    def _(step):
+        ret_step(step, False)
+
+    for step in range(STEPS - LAG, STEPS):
+        for e in range(2):
+            for o in range(3):
+                ret_copy(e, step, o).wait_recv()
     mine = grp == top
     for e in range(2):
         for j in range(n_piece):
             o = jnp.where(base[e][1] > j, 0, jnp.where(base[e][2] > j, 1, 2))
             start = jnp.where(o == 0, base[e][0], jnp.where(o == 1, base[e][1], base[e][2]))
             hop = jnp.where(o == 0, hops[e][0], jnp.where(o == 1, hops[e][1], hops[e][2]))
-            value = ret_in[e, jnp.clip(j - start + hop - 1, 0, STEPS - 1), o]
+            at = jnp.clip(j - start + LAG * (hop - 1), 0, STEPS - 1)
+            value = ret_in[e, at, o]
             out[1 + e, j * PIECE:(j + 1) * PIECE, :] = jnp.where(mine, value, jnp.zeros_like(value))
-
-    for e in range(2):
-        for step in (STEPS - 2, STEPS - 1):
+        stores.append(pltpu.make_async_copy(out.at[1 + e], out_hbm.at[1 + e], out_sem.at[1 + e]))
+        stores[-1].start()
+    for copy in stores:
+        copy.wait()
+
+    for step in range(STEPS - LAG, STEPS):
+        for e in range(2):
             for o in range(3):
                 ret_copy(e, step, o).wait_send()
     for copy in a_copies + x_copies + [over_y] + pending + sib_copies + qr_copies + b_copies:
@@ -346,16 +377,25 @@
     layers, rows, cols = grad_tiles.shape
     blk = 2 * rows
     dma = pltpu.SemaphoreType.DMA
-    vmem = pl.BlockSpec(memory_space=pltpu.VMEM)
-    smem = pl.BlockSpec(memory_space=pltpu.SMEM)
+    hbm = pl.BlockSpec(memory_space=pltpu.HBM)
     n_chunk = rows // CHUNK
     result = pl.pallas_call(
         kernel,
         name="precondition",
         out_shape=jax.ShapeDtypeStruct((CAP, rows, blk), BF16),
-        in_specs=[smem] * 3 + [vmem] * 5,
-        out_specs=vmem,
+        in_specs=[hbm] * 8,
+        out_specs=pl.BlockSpec(memory_space=pl.ANY),
         scratch_shapes=[
+            pltpu.SMEM(layer_group.shape, jnp.int32),
+            pltpu.SMEM(block_counts.shape, jnp.int32),
+            pltpu.SMEM((128,), jnp.int32),
+            pltpu.VMEM((layers, rows, cols), BF16),
+            pltpu.VMEM((layers, rows, cols), BF16),
+            pltpu.VMEM(a_basis.shape, BF16),
+            pltpu.VMEM((layers, blk), F32),
+            pltpu.VMEM((layers, rows), F32),
+            pltpu.VMEM((CAP, rows, blk), BF16),
+            dma((8,)), dma((3,)),
             pltpu.VMEM((layers, rows, cols), BF16),
             pltpu.VMEM((layers, rows, cols), BF16),
             pltpu.VMEM(a_basis.shape, BF16),
@@ -377,10 +417,10 @@
             dma((16,)), dma((16,)),
             dma((2, n_chunk)), dma((2, n_chunk)),
             dma((2, 2)),
-            dma((2, 2, 3)), dma((2, STEPS, 3)),
+            dma((2, LAG, 3)), dma((2, STEPS, 3)),
         ],
         compiler_params=pltpu.CompilerParams(
-            collective_id=0, has_side_effects=True, vmem_limit_bytes=48 * 1024 * 1024
+            collective_id=0, has_side_effects=True, vmem_limit_bytes=63 * 1024 * 1024
         ),
     )(layer_group, block_counts, jnp.asarray(return_tables()), grad_tiles, g_basis, a_basis,
       g_values, a_values)

time: 123 us -> 80 us (0.65)
  Pallas kernels: 113 us -> 75 us
  local copies, waits for them, and re-layouts: 8.72 us -> 3.86 us
    pallas_call x1, Pallas kernels: 113 us -> 75 us  [local(): pl.pallas_call(kernel, name='precondition', out_shape=jax.ShapeDtypeStruc...]
    unnamed x17 -> x1, local copies, waits for them, and re-layouts: 8.72 us -> 3.86 us
where the time goes in v2:
time: 80 us; the launch traced here: 78.9 us
  Pallas kernels  75 us (94%)
  local copies, waits for them, and re-layouts  3.86 us (5%)
    pallas_call x1, Pallas kernels, local(): pl.pallas_call(kernel, name='precondition', out_shape=jax.ShapeDtypeStruc...  75 us
    unnamed x1, local copies, waits for them, and re-layouts  3.86 us

profile of v2, /device:TPU:8, one launch (start us, length us, event | category | flops | bytes accessed | tf_op | source)
XLA Modules:
  0.0 78.9 jit_solution(6675227200154479844)
XLA Ops:
  0.0 75.0 %precondition.1 = bf16[3,512,1024]{2,1,0:T(8,128)(2,1)} custom-call(s32[8]{0:T(128)} %lg_hbm.1, s32[8]{0:T(128)} %bc_hbm.1, s32[128]{0:T(128)} %constant.2.clone.tab_hbm, bf16[8,512,128]{2,1,0:T(8,128)(2,1)} %g_hbm.1, bf16[8,512,128]{2,1,0:T(8,128)(2,1)} %q_hbm.1, bf16[8,32,128]{2,1,0:T(8,128)(2,1)} %a_hbm.1, f32[8,16384]{1,0:T(8,128)} %gv_hbm.1, ...), custom_call_target="tpu_custom_call" | custom-call | tf_op jit(solution)/shard_map/precondition/pallas_call | solution.py:382
  75.0 3.9 %copy.10 = bf16[1,3,512,1024]{3,2,1,0:T(8,128)(2,1)} copy(bf16[1,3,512,1024]{3,2,1,0:T(8,128)(2,1)} %bitcast.1) | data formatting | bytes 6291456

commit v3 on v2

v3 whole, which is shorter than its diff:
```python
import functools

import jax
import jax.numpy as jnp
import numpy as np
from jax import lax
from jax.experimental import pallas as pl
from jax.experimental.pallas import tpu as pltpu
from jax.sharding import PartitionSpec as P

CAP = 3
DAMPING = 0.05
MESH = pl.DeviceIdType.MESH
F32, BF16 = jnp.float32, jnp.bfloat16

NX, NY, NYL, NZ = 4, 2, 2, 8
PEERS = [(1, 0), (0, 1), (3, 0), (1, 1), (2, 0), (3, 1), (2, 1)]
CHUNK = 128
LAGS = (5, 5, 6)
WINDOW = max(LAGS)
SLOTS = 29
FIRST, MORE = 11, 4
TAB = 32
PIECE = 16


HOPS = ((1, 0), (-1, 0), (0, 1))


def routes_to_origin(start):
    found, open_ends = [], [((start,), ())]
    while open_ends:
        nodes, links = open_ends.pop(0)
        for link, (dx, dy) in enumerate(HOPS):
            to = (nodes[-1] // NY + dx) % NX * NY + (nodes[-1] % NY + dy) % NY
            if to == 0:
                found.append((nodes, links + (link,)))
            elif to not in nodes and len(links) < 4:
                open_ends.append((nodes + (to,), links + (link,)))
    return found


def plan(starts, n_piece):
    ways = [routes_to_origin(s) for s in starts]
    busy, left, sent = set(), [n_piece, n_piece], ([], [])
    for slot in range(SLOTS):
        for last in range(3):
            options = []
            for e in range(2):
                for nodes, links in ways[e] if left[e] else []:
                    at, uses = slot, []
                    for k in range(len(links) - 1, -1, -1):
                        uses.append((nodes[k], links[k], at))
                        at -= LAGS[links[k - 1]] if k else 0
                    if links[-1] == last and at >= 0 and not busy.intersection(uses):
                        options.append(((len(links), -left[e], e), e, uses[::-1]))
            if options:
                _, e, uses = min(options, key=lambda o: o[0])
                busy.update(uses)
                left[e] -= 1
                sent[e].append(uses)
    assert not any(left)
    return sent


def return_tables(n_piece):
    n = NX * NY
    table = np.zeros((n, n, n, TAB), np.int32)
    for a in range(1, n):
        for b in range(1, n):
            if a == b:
                continue
            sent = plan((a, b), n_piece)
            for e in range(2):
                for piece, uses in enumerate(sorted(sent[e], key=lambda u: (u[0][2], u[0][1]))):
                    for k, (node, link, slot) in enumerate(uses):
                        code = n_piece + uses[k - 1][1] if k else piece
                        table[a, b, node, slot] += code << (8 * link)
                    table[a, b, 0, piece] += (uses[-1][2] * 4 + uses[-1][1]) << (8 * e)
    return table.reshape(-1)


def kernel(
    lg_hbm, bc_hbm, tab_hbm, g_hbm, q_hbm, a_hbm, gv_hbm, av_hbm, out_hbm,
    lg, bc, tab, g_in, q_in, a_in, gv, av, out, in_sem, out_sem,
    stage_g, stage_q, stage_a, got_g, got_q, a_full, q_full, r_full, inv, acc, s_ref, b_full,
    x_own, ret_out, ret_in,
    x_ss, x_rs, a_ss, a_rs, zs_s, zr_s, sib_ss, sib_rs, qr_ss, qr_rs, b_s, ret_ss, ret_rs,
):
    grp = lax.axis_index("grp")
    mem = lax.axis_index("mem")
    x, yh = grp // 2, grp % 2
    yl, z, core = mem // 16, (mem // 2) % 8, mem % 2
    half, blk = s_ref.shape[1], s_ref.shape[0]
    n_grp = NX * NY

    def peer(dx, dy):
        return {"grp": ((x + dx) % NX) * 2 + (yh + dy) % NY, "mem": mem}

    def mate(dyl, dz, dc):
        row = ((yl + dyl) % NYL) * 16 + ((z + dz) % NZ) * 2 + (core + dc) % 2
        return {"grp": grp, "mem": row}

    sib = mate(0, 0, 1)

    def send(src, dst, ss, rs, device):
        return pltpu.make_async_remote_copy(
            src_ref=src, dst_ref=dst, send_sem=ss, recv_sem=rs,
            device_id=device, device_id_type=MESH,
        )

    barrier = pltpu.get_barrier_semaphore()
    greet = [peer(dx, dy) for dx, dy in PEERS]
    greet += [dict(device, mem=mate(1, 0, 0)["mem"]) for device in greet]
    greet += [sib, mate(1, 0, 0), mate(0, 1, 0), mate(0, -1, 0)]
    for device in greet:
        pl.semaphore_signal(barrier, inc=1, device_id=device, device_id_type=MESH)

    block_row = pl.ds(pl.multiple_of((mem // 2) * blk, blk), blk)
    my_half = pl.ds(pl.multiple_of(core * half, half), half)
    loads = []
    for n, (src, dst) in enumerate((
        (lg_hbm, lg), (a_hbm, a_in), (g_hbm, g_in), (q_hbm, q_in), (bc_hbm, bc),
        (gv_hbm.at[:, block_row], gv), (av_hbm.at[:, my_half], av), (tab_hbm, tab),
    )):
        loads.append(pltpu.make_async_copy(src, dst, in_sem.at[n]))
        loads[-1].start()
    loads[0].wait()

    def pick(cond, value):
        return jnp.where(cond, jnp.int32(value) if isinstance(value, int) else value, jnp.int32(0))

    group = [lg[l] for l in range(n_grp)]
    rank = [
        functools.reduce(lambda s, k: s + pick(group[k] == group[l], 1), range(l), jnp.int32(0))
        for l in range(n_grp)
    ]
    second, third, top, tx, ty = [jnp.int32(0)] * 5
    for l in range(n_grp):
        second = second + pick(rank[l] == 1, l)
        third = third + pick(rank[l] == 2, l)
        top = top + pick(rank[l] == 2, group[l])
    for i in range(n_grp):
        tx = tx + pick(top == i, i // NY)
        ty = ty + pick(top == i, i % NY)
    layer, empties = [], jnp.int32(0)
    helper, helper_x, helper_y = ([jnp.int32(0)] * 2 for _ in range(3))
    my_layer, my_has = jnp.int32(0), jnp.int32(0)
    for i in range(n_grp):
        count, first = jnp.int32(0), jnp.int32(0)
        for l in range(n_grp):
            here = group[l] == i
            count = count + pick(here, 1)
            first = first + pick(jnp.logical_and(here, rank[l] == 0), l)
        empty = count == 0
        layer.append(jnp.where(empty, jnp.where(empties == 0, second, third), first))
        for e in range(2):
            chosen = jnp.logical_and(empty, empties == e)
            helper[e] = helper[e] + pick(chosen, i)
            helper_x[e] = helper_x[e] + pick(chosen, i // NY)
            helper_y[e] = helper_y[e] + pick(chosen, i % NY)
        empties = empties + pick(empty, 1)
        my_layer = my_layer + pick(grp == i, layer[i])
        my_has = my_has + pick(grp == i, jnp.where(empty, jnp.int32(0), jnp.int32(1)))
    loads[1].wait()
    for i in range(n_grp):
        stage_a[i] = a_in[layer[i]]
    pl.semaphore_wait(barrier, len(greet))

    a_rows = a_in.shape[1]
    cols = g_in.shape[2]
    my_cols = pl.ds(pl.multiple_of(grp * cols, cols), cols)

    def piece(yl_, z_, core_):
        start = ((yl_ % NYL) * 16 + (z_ % NZ) * 2 + core_) * a_rows
        return pl.ds(pl.multiple_of(start, a_rows), a_rows)

    own_piece = piece(yl, z, core)
    a_copies = []
    for dyl in range(2):
        for n, (dx, dy) in enumerate(PEERS + [(0, 0)] * dyl):
            device = dict(peer(dx, dy), mem=mate(dyl, 0, 0)["mem"])
            a_copies.append(send(stage_a.at[device["grp"]], a_full.at[own_piece, my_cols],
                                 a_ss.at[dyl, n], a_rs.at[dyl, n], device))
            a_copies[-1].start()
    a_full[own_piece, my_cols] = stage_a[grp]

    n_chunk = g_in.shape[1] // CHUNK
    x_copies = []
    moves = ((g_in, stage_g, got_g, loads[2]), (q_in, stage_q, got_q, loads[3]))

    def exchange(more):
        for count in range(len(x_copies), min(len(x_copies) + more, 14 * n_chunk)):
            c, t, n = count // 14, count // 7 % 2, count % 7
            whole, stage, got, load = moves[t]
            rows = pl.ds(c * CHUNK, CHUNK)
            if n == 0:
                if c == 0:
                    load.wait()
                for i in range(n_grp):
                    stage[i, rows] = whole[layer[i], rows]
                got[grp, rows] = stage[grp, rows]
            device = peer(*PEERS[n])
            copy = send(stage.at[device["grp"], rows], got.at[grp, rows],
                        x_ss.at[c, t, n], x_rs.at[c, t, n], device)
            copy.start()
            x_copies.append(copy)

    exchange(FIRST)

    pending = []
    sib_copies = []

    def to_sib(rows):
        n = len(sib_copies)
        copy = send(a_full.at[rows], a_full.at[rows], sib_ss.at[n], sib_rs.at[n], sib)
        copy.start()
        sib_copies.append(copy)

    def along_z(way, step, j, rows):
        copy = send(a_full.at[rows], a_full.at[rows], zs_s.at[way, step, j], zr_s.at[way, step, j],
                    mate(0, 1 - 2 * way, 0))
        copy.start()
        pending.append(copy)
        return copy

    for copy in a_copies[:7]:
        copy.wait_recv()
    ring = {}
    for way in range(2):
        ring[way, 0, 0] = along_z(way, 0, 0, own_piece)
    to_sib(own_piece)
    exchange(MORE)
    other_piece = piece(yl + 1, z, core)
    for copy in a_copies[7:]:
        copy.wait_recv()
    for way in range(2):
        ring[way, 0, 1] = along_z(way, 0, 1, other_piece)
    to_sib(other_piece)
    exchange(MORE)
    for load in loads[4:7]:
        load.wait()
    my_count = jnp.int32(0)
    for l in range(n_grp):
        my_count = my_count + pick(my_layer == l, bc[l])
    live = my_count > mem // 2

    e_row, a_row = gv[0:1, :], av[0:1, :]
    for l in range(1, n_grp):
        e_row = jnp.where(my_layer == l, gv[l:l + 1, :], e_row)
        a_row = jnp.where(my_layer == l, av[l:l + 1, :], a_row)
    for t in range(blk // 128):
        tile = jnp.broadcast_to(e_row[:, t * 128:(t + 1) * 128], (128, 128)).T
        for u in range(half // 128):
            denom = tile * a_row[:, u * 128:(u + 1) * 128] + DAMPING
            inv[t * 128:(t + 1) * 128, u * 128:(u + 1) * 128] = 1.0 / denom

    for step in range(1, 5):
        for j in range(2):
            for way in range(2):
                if (way, step - 1, j) not in ring:
                    continue
                ring[way, step - 1, j].wait_recv()
                came = piece(yl + j, z - step * (1 - 2 * way), core)
                if step < 3 or (step == 3 and j == way):
                    ring[way, step, j] = along_z(way, step, j, came)
                to_sib(came)
                exchange(MORE)
    exchange(14 * n_chunk)
    for copy in sib_copies:
        copy.wait_recv()

    qr_copies = []
    sib_half = pl.ds(pl.multiple_of((1 - core) * half, half), half)
    done = half - CHUNK

    def across(start, size):
        return [pl.ds(pl.multiple_of(who * half + start, CHUNK), size) for who in (core, 1 - core)]

    def rotate(start, size, t):
        rows = across(start, size)
        q = jnp.concatenate([q_full[r, t * 256:(t + 1) * 256] for r in rows], axis=0)
        turned = jnp.concatenate([r_full[r, my_half] for r in rows], axis=0)
        return lax.dot_general(q, turned, (((0,), (0,)), ((), ())), preferred_element_type=F32)

    def to_other_core(t, c, ref):
        copy = send(ref, ref, qr_ss.at[t, c], qr_rs.at[t, c], sib)
        copy.start()
        qr_copies.append(copy)

    for c in range(n_chunk):
        rows = pl.ds(c * CHUNK, CHUNK)
        abs_rows = across(c * CHUNK, CHUNK)[0]
        for copy in x_copies[c * 14:c * 14 + 7]:
            copy.wait_recv()
        g_rows = jnp.concatenate([got_g[i, rows] for i in range(n_grp)], axis=1)
        for n in range(blk // 256):
            r_full[abs_rows, n * 256:(n + 1) * 256] = jnp.dot(
                g_rows, a_full[:, n * 256:(n + 1) * 256], preferred_element_type=F32
            ).astype(BF16)
        to_other_core(1, c, r_full.at[abs_rows, sib_half])
        if c == n_chunk - 1:
            for copy in qr_copies[:-1]:
                copy.wait_recv()
            for t in range(blk // 256):
                acc[t * 256:(t + 1) * 256, :] = rotate(0, done, t)
        for copy in x_copies[c * 14 + 7:c * 14 + 14]:
            copy.wait_recv()
        q_full[abs_rows, :] = jnp.concatenate([got_q[i, rows] for i in range(n_grp)], axis=1)
        to_other_core(0, c, q_full.at[abs_rows])
    for copy in qr_copies[-2:]:
        copy.wait_recv()

    for t in range(blk // 256):
        cut = slice(t * 256, (t + 1) * 256)
        rotated = acc[cut, :] + rotate(done, CHUNK, t)
        s_ref[cut, :] = (rotated * inv[cut, :]).astype(BF16)

    b_copies = []
    for t in range(4):
        who = 1 - core if t < 2 else core
        rows = pl.ds(pl.multiple_of(who * half + (t % 2) * 256, 256), 256)
        b_full[rows, my_half] = jnp.dot(
            q_full[rows, :], s_ref[...], preferred_element_type=F32
        ).astype(BF16)
        if t < 2:
            copy = send(b_full.at[rows, my_half], b_full.at[rows, my_half], b_s.at[0, t],
                        b_s.at[1, t], sib)
            copy.start()
            b_copies.append(copy)
    for copy in b_copies:
        copy.wait_recv()

    loads[7].wait()
    def apart(a, b, n):
        return jnp.where(a < b, a - b + n, a - b)

    here = apart(x, tx, NX) * NY + apart(yh, ty, NY)
    place = [apart(helper_x[e], tx, NX) * NY + apart(helper_y[e], ty, NY) for e in range(2)]
    case = (place[0] * n_grp + place[1]) * n_grp
    n_piece = half // PIECE
    ways = [peer(*hop) for hop in HOPS]

    def ret_copy(slot, o):
        return send(ret_out.at[slot, o], ret_in.at[slot, o], ret_ss.at[slot % WINDOW, o],
                    ret_rs.at[slot, o], ways[o])

    def ret_slot(slot, came, reuse):
        word = tab[(case + here) * TAB + slot]
        for o in came:
            ret_copy(slot - LAGS[o], o).wait_recv()
        for o in range(3):
            code = (word >> (8 * o)) & 255
            value = x_own[jnp.minimum(code, n_piece - 1)]
            for r in came:
                value = jnp.where(code == n_piece + r, ret_in[slot - LAGS[r], r], value)
            ret_out[slot, o] = value
            if reuse:
                ret_copy(slot - WINDOW, o).wait_send()
            ret_copy(slot, o).start()

    for t in range(half // 128):
        rows = pl.ds(pl.multiple_of(core * half + t * 128, 128), 128)
        left = b_full[rows, :]
        for n in range(blk // 256):
            update = lax.dot_general(left, a_full[n * 256:(n + 1) * 256, :],
                                     (((1,), (1,)), ((), ())), preferred_element_type=F32)
            update = jnp.where(live, update, 0.0).astype(BF16)
            per = 128 // PIECE
            x_own[t * per:(t + 1) * per, :, n * 256:(n + 1) * 256] = update.reshape(per, PIECE, 256)
        ret_slot(t, [o for o in range(3) if LAGS[o] <= t], False)
    for slot in range(half // 128, WINDOW):
        ret_slot(slot, [o for o in range(3) if LAGS[o] <= slot], False)

    keep = my_has > 0
    for j in range(n_piece):
        value = x_own[j]
        out[0, j * PIECE:(j + 1) * PIECE, :] = jnp.where(keep, value, jnp.zeros_like(value))
    stores = [pltpu.make_async_copy(out.at[0], out_hbm.at[0], out_sem.at[0])]
    stores[0].start()

    @pl.loop(WINDOW, SLOTS)
    def _(slot):
        ret_slot(slot, range(3), True)

    for o in range(3):
        for slot in range(SLOTS - LAGS[o], SLOTS):
            ret_copy(slot, o).wait_recv()
    mine = grp == top
    for e in range(2):
        for j in range(n_piece):
            code = (tab[case * TAB + j] >> (8 * e)) & 255
            value = ret_in[jnp.minimum(code >> 2, SLOTS - 1), jnp.minimum(code & 3, 2)]
            out[1 + e, j * PIECE:(j + 1) * PIECE, :] = jnp.where(mine, value, jnp.zeros_like(value))
        stores.append(pltpu.make_async_copy(out.at[1 + e], out_hbm.at[1 + e], out_sem.at[1 + e]))
        stores[-1].start()
    for copy in stores:
        copy.wait()

    for slot in range(SLOTS - WINDOW, SLOTS):
        for o in range(3):
            ret_copy(slot, o).wait_send()
    for copy in a_copies + x_copies + pending + sib_copies + qr_copies + b_copies:
        copy.wait_send()


def local(grad_tiles, g_basis, a_basis, g_values, a_values, layer_group, block_counts):
    layers, rows, cols = grad_tiles.shape
    blk = 2 * rows
    dma = pltpu.SemaphoreType.DMA
    table = return_tables(rows // PIECE)
    hbm = pl.BlockSpec(memory_space=pltpu.HBM)
    n_chunk = rows // CHUNK
    result = pl.pallas_call(
        kernel,
        name="precondition",
        out_shape=jax.ShapeDtypeStruct((CAP, rows, blk), BF16),
        in_specs=[hbm] * 8,
        out_specs=pl.BlockSpec(memory_space=pl.ANY),
        scratch_shapes=[
            pltpu.SMEM(layer_group.shape, jnp.int32),
            pltpu.SMEM(block_counts.shape, jnp.int32),
            pltpu.SMEM(table.shape, jnp.int32),
            pltpu.VMEM((layers, rows, cols), BF16),
            pltpu.VMEM((layers, rows, cols), BF16),
            pltpu.VMEM(a_basis.shape, BF16),
            pltpu.VMEM((layers, blk), F32),
            pltpu.VMEM((layers, rows), F32),
            pltpu.VMEM((CAP, rows, blk), BF16),
            dma((8,)), dma((3,)),
            pltpu.VMEM((layers, rows, cols), BF16),
            pltpu.VMEM((layers, rows, cols), BF16),
            pltpu.VMEM(a_basis.shape, BF16),
            pltpu.VMEM((layers, rows, cols), BF16),
            pltpu.VMEM((layers, rows, cols), BF16),
            pltpu.VMEM((blk, blk), BF16),
            pltpu.VMEM((blk, blk), BF16),
            pltpu.VMEM((blk, blk), BF16),
            pltpu.VMEM((blk, rows), F32),
            pltpu.VMEM((blk, rows), F32),
            pltpu.VMEM((blk, rows), BF16),
            pltpu.VMEM((blk, blk), BF16),
            pltpu.VMEM((rows // PIECE, PIECE, blk), BF16),
            pltpu.VMEM((SLOTS, 3, PIECE, blk), BF16),
            pltpu.VMEM((SLOTS, 3, PIECE, blk), BF16),
            dma((n_chunk, 2, 7)), dma((n_chunk, 2, 7)),
            dma((2, 8)), dma((2, 8)),
            dma((2, 4, 2)), dma((2, 4, 2)),
            dma((16,)), dma((16,)),
            dma((2, n_chunk)), dma((2, n_chunk)),
            dma((2, 2)),
            dma((WINDOW, 3)), dma((SLOTS, 3)),
        ],
        compiler_params=pltpu.CompilerParams(
            collective_id=0, has_side_effects=True, vmem_limit_bytes=63 * 1024 * 1024
        ),
    )(layer_group, block_counts, jnp.asarray(table), grad_tiles, g_basis, a_basis,
      g_values, a_values)
    return result[None]


def solution(mesh):
    in_specs = (
        P(None, "mem", "grp"),
        P(None, "mem", "grp"),
        P(None, "mem", "grp"),
        P(),
        P(),
        P(),
        P(),
    )
    out_specs = P("grp", None, "mem", None)
    return jax.shard_map(local, mesh=mesh, in_specs=in_specs, out_specs=out_specs, check_vma=False)
```

time: 80 us -> 74.1 us (0.926); the launches traced: 78.9 us -> 73.8 us
  Pallas kernels: 75 us -> 70 us
    pallas_call x1, Pallas kernels: 75 us -> 70 us  [local(): pl.pallas_call(kernel, name='precondition', out_shape=jax.ShapeDtypeStruc...]
where the time goes in v3:
time: 74.1 us; the launch traced here: 73.8 us
  Pallas kernels  70 us (94%)
  local copies, waits for them, and re-layouts  3.86 us (5%)
    pallas_call x1, Pallas kernels, local(): pl.pallas_call(kernel, name='precondition', out_shape=jax.ShapeDtypeStruc...  70 us
    unnamed x1, local copies, waits for them, and re-layouts  3.86 us

profile of v3, /device:TPU:8, one launch (start us, length us, event | category | flops | bytes accessed | tf_op | source)
XLA Modules:
  0.0 73.8 jit_solution(5710549284930473777)
XLA Ops:
  0.0 70.0 %precondition.1 = bf16[3,512,1024]{2,1,0:T(8,128)(2,1)} custom-call(s32[8]{0:T(128)} %lg_hbm.1, s32[8]{0:T(128)} %bc_hbm.1, s32[16384]{0:T(1024)} %constant.2.clone.tab_hbm, bf16[8,512,128]{2,1,0:T(8,128)(2,1)} %g_hbm.1, bf16[8,512,128]{2,1,0:T(8,128)(2,1)} %q_hbm.1, bf16[8,32,128]{2,1,0:T(8,128)(2,1)} %a_hbm.1, f32[8,16384]{1,0:T(8,128)} %gv_hbm.1, ...), custom_call_target="tpu_custom_call" | custom-call | tf_op jit(solution)/shard_map/precondition/pallas_call | solution.py:414
  70.0 3.9 %copy.10 = bf16[1,3,512,1024]{3,2,1,0:T(8,128)(2,1)} copy(bf16[1,3,512,1024]{3,2,1,0:T(8,128)(2,1)} %bitcast.1) | data formatting | bytes 6291456

commit v4 on v3

--- a/solution.py
+++ b/solution.py
@@ -14,7 +14,7 @@
 F32, BF16 = jnp.float32, jnp.bfloat16
 
 NX, NY, NYL, NZ = 4, 2, 2, 8
-PEERS = [(1, 0), (0, 1), (3, 0), (1, 1), (2, 0), (3, 1), (2, 1)]
+PEERS = [(2, 1), (1, 0), (0, 1), (3, 0), (2, 0), (1, 1), (3, 1)]
 CHUNK = 128
 LAGS = (5, 5, 6)
 WINDOW = max(LAGS)
@@ -81,8 +81,8 @@
 
 
 def kernel(
-    lg_hbm, bc_hbm, tab_hbm, g_hbm, q_hbm, a_hbm, gv_hbm, av_hbm, out_hbm,
-    lg, bc, tab, g_in, q_in, a_in, gv, av, out, in_sem, out_sem,
+    lg_hbm, bc_hbm, tab_hbm, g_hbm, q_hbm, a_hbm, gv_hbm, av_hbm, out,
+    lg, bc, tab, g_in, q_in, a_in, gv, av, in_sem,
     stage_g, stage_q, stage_a, got_g, got_q, a_full, q_full, r_full, inv, acc, s_ref, b_full,
     x_own, ret_out, ret_in,
     x_ss, x_rs, a_ss, a_rs, zs_s, zr_s, sib_ss, sib_rs, qr_ss, qr_rs, b_s, ret_ss, ret_rs,
@@ -376,8 +376,6 @@
     for j in range(n_piece):
         value = x_own[j]
         out[0, j * PIECE:(j + 1) * PIECE, :] = jnp.where(keep, value, jnp.zeros_like(value))
-    stores = [pltpu.make_async_copy(out.at[0], out_hbm.at[0], out_sem.at[0])]
-    stores[0].start()
 
     @pl.loop(WINDOW, SLOTS)
     def _(slot):
@@ -392,10 +390,6 @@
             code = (tab[case * TAB + j] >> (8 * e)) & 255
             value = ret_in[jnp.minimum(code >> 2, SLOTS - 1), jnp.minimum(code & 3, 2)]
             out[1 + e, j * PIECE:(j + 1) * PIECE, :] = jnp.where(mine, value, jnp.zeros_like(value))
-        stores.append(pltpu.make_async_copy(out.at[1 + e], out_hbm.at[1 + e], out_sem.at[1 + e]))
-        stores[-1].start()
-    for copy in stores:
-        copy.wait()
 
     for slot in range(SLOTS - WINDOW, SLOTS):
         for o in range(3):
@@ -416,7 +410,7 @@
         name="precondition",
         out_shape=jax.ShapeDtypeStruct((CAP, rows, blk), BF16),
         in_specs=[hbm] * 8,
-        out_specs=pl.BlockSpec(memory_space=pl.ANY),
+        out_specs=pl.BlockSpec(memory_space=pltpu.VMEM),
         scratch_shapes=[
             pltpu.SMEM(layer_group.shape, jnp.int32),
             pltpu.SMEM(block_counts.shape, jnp.int32),
@@ -426,8 +420,7 @@
             pltpu.VMEM(a_basis.shape, BF16),
             pltpu.VMEM((layers, blk), F32),
             pltpu.VMEM((layers, rows), F32),
-            pltpu.VMEM((CAP, rows, blk), BF16),
-            dma((8,)), dma((3,)),
+            dma((8,)),
             pltpu.VMEM((layers, rows, cols), BF16),
             pltpu.VMEM((layers, rows, cols), BF16),
             pltpu.VMEM(a_basis.shape, BF16),
@@ -452,10 +445,11 @@
             dma((WINDOW, 3)), dma((SLOTS, 3)),
         ],
         compiler_params=pltpu.CompilerParams(
-            collective_id=0, has_side_effects=True, vmem_limit_bytes=63 * 1024 * 1024
+            collective_id=0, has_side_effects=True, vmem_limit_bytes=48 * 1024 * 1024
         ),
-    )(layer_group, block_counts, jnp.asarray(table), grad_tiles, g_basis, a_basis,
-      g_values, a_values)
+    )(*(pltpu.with_memory_space_constraint(array, pltpu.HBM) for array in (
+        layer_group, block_counts, jnp.asarray(table), grad_tiles, g_basis, a_basis, g_values,
+        a_values)))
     return result[None]
 
 

time: 74.1 us -> 70.1 us (0.946)
  local copies, waits for them, and re-layouts: 3.86 us -> 1.67 us
  Pallas kernels: 70 us -> 68.3 us
    unnamed x1, local copies, waits for them, and re-layouts: 3.86 us -> 1.67 us
    pallas_call x1, Pallas kernels: 70 us -> 68.3 us  [local(): pl.pallas_call(kernel, name='precondition', out_shape=jax.ShapeDtypeStruc...]
where the time goes in v4:
time: 70.1 us; the launch traced here: 70 us
  Pallas kernels  68.3 us (97%)
  local copies, waits for them, and re-layouts  1.67 us (2%)
    pallas_call x1, Pallas kernels, local(): pl.pallas_call(kernel, name='precondition', out_shape=jax.ShapeDtypeStruc...  68.3 us
    unnamed x1, local copies, waits for them, and re-layouts  1.67 us

profile of v4, /device:TPU:8, one launch (start us, length us, event | category | flops | bytes accessed | tf_op | source)
XLA Modules:
  0.0 70.0 jit_solution(11803820243433286021)
XLA Ops:
  0.0 68.3 %precondition.1 = bf16[3,512,1024]{2,1,0:T(8,128)(2,1)S(1)} custom-call(s32[8]{0:T(128)} %lg_hbm.1, s32[8]{0:T(128)} %bc_hbm.1, s32[16384]{0:T(1024)} %constant.2.clone.tab_hbm, bf16[8,512,128]{2,1,0:T(8,128)(2,1)} %g_hbm.1, bf16[8,512,128]{2,1,0:T(8,128)(2,1)} %q_hbm.1, bf16[8,32,128]{2,1,0:T(8,128)(2,1)} %a_hbm.1, f32[8,16384]{1,0:T(8,128)} %gv_hbm.1, ...), custom_call_target="tpu_custom_call" | custom-call | tf_op jit(solution)/shard_map/precondition/pallas_call | solution.py:408
  68.4 1.7 %copy.10 = bf16[1,3,512,1024]{3,2,1,0:T(8,128)(2,1)} copy(bf16[1,3,512,1024]{3,2,1,0:T(8,128)(2,1)S(1)} %bitcast.1) | data formatting | bytes 6291456

commit v5 on v4

--- a/solution.py
+++ b/solution.py
@@ -15,11 +15,12 @@
 
 NX, NY, NYL, NZ = 4, 2, 2, 8
 PEERS = [(2, 1), (1, 0), (0, 1), (3, 0), (2, 0), (1, 1), (3, 1)]
+FAR = [(2, 1), (1, 1), (3, 1), (0, 1), (2, 0), (1, 0), (3, 0)]
 CHUNK = 128
 LAGS = (5, 5, 6)
 WINDOW = max(LAGS)
 SLOTS = 29
-FIRST, MORE = 11, 4
+FIRST, MORE = 18, 6
 TAB = 32
 PIECE = 16
 
@@ -178,7 +179,7 @@
     own_piece = piece(yl, z, core)
     a_copies = []
     for dyl in range(2):
-        for n, (dx, dy) in enumerate(PEERS + [(0, 0)] * dyl):
+        for n, (dx, dy) in enumerate(FAR + [(0, 0)] * dyl):
             device = dict(peer(dx, dy), mem=mate(dyl, 0, 0)["mem"])
             a_copies.append(send(stage_a.at[device["grp"]], a_full.at[own_piece, my_cols],
                                  a_ss.at[dyl, n], a_rs.at[dyl, n], device))
@@ -381,14 +382,19 @@
     def _(slot):
         ret_slot(slot, range(3), True)
 
+    spots = []
+    for j in range(n_piece):
+        word = tab[case * TAB + j]
+        for e in range(2):
+            code = (word >> (8 * e)) & 255
+            spots.append((jnp.minimum(code >> 2, SLOTS - 1), jnp.minimum(code & 3, 2)))
+    mine = grp == top
     for o in range(3):
         for slot in range(SLOTS - LAGS[o], SLOTS):
             ret_copy(slot, o).wait_recv()
-    mine = grp == top
     for e in range(2):
         for j in range(n_piece):
-            code = (tab[case * TAB + j] >> (8 * e)) & 255
-            value = ret_in[jnp.minimum(code >> 2, SLOTS - 1), jnp.minimum(code & 3, 2)]
+            value = ret_in[spots[j * 2 + e]]
             out[1 + e, j * PIECE:(j + 1) * PIECE, :] = jnp.where(mine, value, jnp.zeros_like(value))
 
     for slot in range(SLOTS - WINDOW, SLOTS):

time: 70.1 us -> 70 us (level)
  no operation moved by 1% of the time
where the time goes in v5:
time: 70 us; the launch traced here: 69.9 us
  Pallas kernels  68.2 us (97%)
  local copies, waits for them, and re-layouts  1.67 us (2%)
    pallas_call x1, Pallas kernels, local(): pl.pallas_call(kernel, name='precondition', out_shape=jax.ShapeDtypeStruc...  68.2 us
    unnamed x1, local copies, waits for them, and re-layouts  1.67 us

profile of v5, /device:TPU:8, one launch (start us, length us, event | category | flops | bytes accessed | tf_op | source)
XLA Modules:
  0.0 69.9 jit_solution(10926568018138694632)
XLA Ops:
  0.0 68.2 %precondition.1 = bf16[3,512,1024]{2,1,0:T(8,128)(2,1)S(1)} custom-call(s32[8]{0:T(128)} %lg_hbm.1, s32[8]{0:T(128)} %bc_hbm.1, s32[16384]{0:T(1024)} %constant.2.clone.tab_hbm, bf16[8,512,128]{2,1,0:T(8,128)(2,1)} %g_hbm.1, bf16[8,512,128]{2,1,0:T(8,128)(2,1)} %q_hbm.1, bf16[8,32,128]{2,1,0:T(8,128)(2,1)} %a_hbm.1, f32[8,16384]{1,0:T(8,128)} %gv_hbm.1, ...), custom_call_target="tpu_custom_call" | custom-call | tf_op jit(solution)/shard_map/precondition/pallas_call | solution.py:414
  68.2 1.7 %copy.10 = bf16[1,3,512,1024]{3,2,1,0:T(8,128)(2,1)} copy(bf16[1,3,512,1024]{3,2,1,0:T(8,128)(2,1)S(1)} %bitcast.1) | data formatting | bytes 6291456
